TPU v7x, 32 devices: a whole 2x2x4 slice. The times are simulated.
32 devices in a mesh: sections: 2 (over x), tx: 16 (over z, y, core).
Axes of the slice: x: 2, y: 2, z: 4, core: 2. Of those that a mesh axis runs over, the one named last changes fastest.
Arguments:
- positions: float32 [2, 32768], P(None, ('sections', 'tx')), parts along dimension 1, may hold values from 0 to 128, as said below
- counts: int32 [256], P(('sections', 'tx')), parts along dimension 0, may hold values from 1 to 128, as said below
- ligands: float32 [32768, 128], P(('sections', 'tx')), parts along dimension 0, may hold values from 0.1 to 10
- receptors: float32 [32768, 128], P(('sections', 'tx')), parts along dimension 0, may hold values from 0.1 to 10
- lig_of_pair: int32 [128], replicated, may hold values from 0 to 127
- rec_of_pair: int32 [128], replicated, may hold values from 0 to 127
Outputs:
- received: float32 [32768, 128], P(('sections', 'tx')), parts along dimension 0
There are 2 independent parts, one for each index of `sections`. A program takes and returns all parts, laid end to end along the dimension named above; an argument that names none is the same for every part. Nothing has to cross between parts.
Inputs may be any that keep to these rules, and one draw needn't show every extreme that they name: `positions`: cell slot r has its first coordinate in [r // 128, r // 128 + 1) and its second in [0, 32). `counts`: the live cells of a block are its first slots; the last block is full in every draw.
All inputs are finite; a program needn't handle non-finite values.
Results may differ from a plain program's by a relative error of at most 0.00022.
Values sent between devices are 32-bit elements; how exact they have to be, the bound alone decides.
A program may use at most 64 MiB of HBM per device.

v0:
```python
import jax
import jax.numpy as jnp
from jax import lax
from jax.sharding import PartitionSpec as P

BLK = 128
HB = 2
ITERS = 3


entropy = 0.5
relaxation = 1.0


def extended_2(x, sides, width):
    for axis, dim in sides:
        size, length = (lax.axis_size(axis), x.shape[dim])
        up = [(i, (i + 1) % size) for i in range(size - 1)]
        down = [(j, i) for i, j in up]
        last = lax.slice_in_dim(x, length - width, length, axis=dim)
        first = lax.slice_in_dim(x, 0, width, axis=dim)
        before = lax.ppermute(last, axis, up)
        after = lax.ppermute(first, axis, down)
        x = jnp.concatenate([before, x, after], axis=dim)
    return x


def pair_kernel(row_x, row_y, col_x, col_y):
    radius = float(HB)
    scaled_sq = (jnp.square(row_x - col_x) + jnp.square(row_y - col_y)) / (radius * radius)
    tapered = jnp.square(jnp.maximum(1.0 - scaled_sq, 0.0))
    return tapered * jnp.exp(-scaled_sq / entropy)


def body(positions, counts, ligands, receptors, lig_of_pair, rec_of_pair):
    cells_dev = positions.shape[1]
    nblock = counts.shape[0]
    pair_count = lig_of_pair.shape[0]
    rim_rows = HB * BLK
    band_size = 2 * HB + 1
    live_mask = (
        (jnp.arange(BLK, dtype=jnp.int32)[None, :] < counts[:, None])
        .astype(jnp.float32)
        .reshape(cells_dev, 1)
    )
    pick_lig = (
        jnp.arange(ligands.shape[1], dtype=jnp.int32)[:, None] == lig_of_pair[None, :]
    ).astype(jnp.float32)
    pick_rec = (
        jnp.arange(receptors.shape[1], dtype=jnp.int32)[:, None] == rec_of_pair[None, :]
    ).astype(jnp.float32)
    supply = jnp.dot(
        ligands, pick_lig, precision=lax.Precision.HIGHEST, preferred_element_type=jnp.float32
    )
    demand = jnp.dot(
        receptors, pick_rec, precision=lax.Precision.HIGHEST, preferred_element_type=jnp.float32
    )
    log_supply = jnp.log(supply)
    log_demand = jnp.log(demand)
    extended = extended_2(positions, (("tx", 1),), rim_rows)
    pos_win = jnp.stack(
        [extended[:, slot_k * BLK : slot_k * BLK + cells_dev] for slot_k in range(band_size)], 0
    )
    own_x = positions[0].reshape(nblock, 1, BLK, 1)
    own_y = positions[1].reshape(nblock, 1, BLK, 1)
    near_x = pos_win[:, 0].reshape(band_size, nblock, BLK).transpose(1, 0, 2)[:, :, None, :]
    near_y = pos_win[:, 1].reshape(band_size, nblock, BLK).transpose(1, 0, 2)[:, :, None, :]
    band_tiles = pair_kernel(own_x, own_y, near_x, near_y)
    left_tile = pair_kernel(
        extended[0, :rim_rows][:, None],
        extended[1, :rim_rows][:, None],
        positions[0, :rim_rows][None, :],
        positions[1, :rim_rows][None, :],
    )
    right_tile = pair_kernel(
        extended[0, -rim_rows:][:, None],
        extended[1, -rim_rows:][:, None],
        positions[0, -rim_rows:][None, :],
        positions[1, -rim_rows:][None, :],
    )
    cached = (band_tiles, (left_tile, right_tile))

    def apply_tiles(band_tiles, values_ext):
        val_win = jnp.stack(
            [values_ext[slot_k * BLK : slot_k * BLK + cells_dev] for slot_k in range(band_size)], 0
        )
        val_win = val_win.reshape(band_size, nblock, BLK, pair_count)
        result = jnp.einsum(
            "bkij,kbjp->bip",
            band_tiles,
            val_win,
            precision=lax.Precision.HIGHEST,
            preferred_element_type=jnp.float32,
        )
        return result.reshape(cells_dev, pair_count)

    def neighbour_sum(values):
        band_tiles, edge_tiles = cached
        values_ext = extended_2(values, (("tx", 0),), rim_rows)
        return apply_tiles(band_tiles, values_ext)

    factor = relaxation / (relaxation + entropy)
    recv_pot = jnp.zeros((cells_dev, pair_count), jnp.float32)
    gathered = jnp.zeros((cells_dev, pair_count), jnp.float32)
    for rounds in range(ITERS):
        sent_mass = neighbour_sum(live_mask * jnp.exp(recv_pot / entropy))
        send_pot = (
            live_mask * factor * entropy * (log_supply - jnp.log(sent_mass + 1.0 - live_mask))
        )
        gathered = neighbour_sum(live_mask * jnp.exp(send_pot / entropy))
        recv_pot = live_mask * factor * entropy * (log_demand - jnp.log(gathered + 1.0 - live_mask))
    flux_out = live_mask * jnp.exp(recv_pot / entropy) * gathered
    global_sums = lax.psum((jnp.sum(flux_out, axis=0), jnp.sum(counts.astype(jnp.float32))), "tx")
    return flux_out * (global_sums[1] / global_sums[0])[None, :]


def solution(mesh):
    in_specs = (
        P(None, ("sections", "tx")),
        P(("sections", "tx")),
        P(("sections", "tx"), None),
        P(("sections", "tx"), None),
        P(),
        P(),
    )
    out_specs = P(("sections", "tx"), None)
    return jax.shard_map(body, mesh=mesh, in_specs=in_specs, out_specs=out_specs, check_vma=False)
```

profile of v0, /device:TPU:0, one launch (start us, length us, event | category | flops | bytes accessed | tf_op | source)
XLA Modules:
  0.0 187.2 jit_solution(6196028176430558850)
XLA Ops:
  0.8 1.3 collective-permute-start.3
  2.1 3.0 %collective-permute-start.2 = (f32[256,128]{0,1:T(8,128)S(1)}, f32[256,128]{0,1:T(8,128)S(1)}, u32[]{:S(2)}, u32[]{:S(2)}) collective-permute-start(f32[256,128]{0,1:T(8,128)S(1)} %mul.54), channel_id=1, source_target_pairs={{0,1},{1,2},{2,3},{3,4},{4,5},{5,6},{6,7},{7,8},{8,9},{9,10},{10,1... | collective-permute-start | bytes 393224 | tf_op jit(solution)/shard_map/ppermute | solution.py:22
  5.9 4.5 %collective-permute-start = (f32[2,256]{1,0:T(2,128)S(1)}, f32[2,256]{1,0:T(2,128)S(1)}, u32[]{:S(2)}, u32[]{:S(2)}) collective-permute-start(f32[2,256]{1,0:T(2,128)S(1)} %get-tuple-element.58), channel_id=1, source_target_pairs={{0,1},{1,2},{2,3},{3,4},{4,5},{5,6},{6,7},{7,8},{8,9},{9,10},{10,1... | collective-permute-start | bytes 6152 | tf_op jit(solution)/shard_map/ppermute | solution.py:22
  10.4 1.3 collective-permute-start.1
  20.1 5.6 %fusion.17 = f32[8,128,128]{2,1,0:T(8,128)S(1)} fusion(f32[5,8,128,128]{3,2,0,1:T(8,128)} %constant_dynamic-update-slice_fusion.9, f32[8,5,128]{2,1,0:T(8,128)S(1)} %copy.8, f32[8,128]{1,0:T(8,128)S(1)} %bitcast.152, f32[8,5,128]{2,1,0:T(8,128)S(1)} %copy.7, f32[8,128]{1,0:T(8,128)S(1)} %bitcast.146), kind=kOutput, calls=%fused_computation.20 | convolution fusion | flops 1014628352 | bytes 3194880 | tf_op jit(solution)/shard_map/bkij,kbjp->bip/dot_general | solution.py:88
  26.6 1.3 collective-permute-start.5
  27.9 4.1 %collective-permute-start.4 = (f32[256,128]{0,1:T(8,128)S(1)}, f32[256,128]{0,1:T(8,128)S(1)}, u32[]{:S(2)}, u32[]{:S(2)}) collective-permute-start(f32[256,128]{0,1:T(8,128)S(1)} %get-tuple-element.50), channel_id=1, source_target_pairs={{0,1},{1,2},{2,3},{3,4},{4,5},{5,6},{6,7},{7,8},{8,9},{9,10},{10,1... | collective-permute-start | bytes 393224 | tf_op jit(solution)/shard_map/ppermute | solution.py:22
  36.5 1.2 copy.60
  41.1 5.7 %fusion.16 = f32[8,128,128]{2,1,0:T(8,128)S(1)} fusion(f32[5,8,128,128]{3,2,0,1:T(8,128)} %constant_dynamic-update-slice_fusion.13, f32[8,5,128]{2,1,0:T(8,128)S(1)} %copy.8, f32[8,128]{1,0:T(8,128)S(1)} %bitcast.153, f32[8,5,128]{2,1,0:T(8,128)S(1)} %copy.7, f32[8,128]{1,0:T(8,128)S(1)} %bitcast.147), kind=kOutput, calls=%fused_computation.19 | convolution fusion | flops 1014628352 | bytes 3194880 | tf_op jit(solution)/shard_map/bkij,kbjp->bip/dot_general | solution.py:88
  47.6 1.3 collective-permute-start.7
  48.9 6.6 %collective-permute-start.6 = (f32[256,128]{0,1:T(8,128)S(1)}, f32[256,128]{0,1:T(8,128)S(1)}, u32[]{:S(2)}, u32[]{:S(2)}) collective-permute-start(f32[256,128]{0,1:T(8,128)S(1)} %get-tuple-element.46), channel_id=1, source_target_pairs={{0,1},{1,2},{2,3},{3,4},{4,5},{5,6},{6,7},{7,8},{8,9},{9,10},{10,1... | collective-permute-start | bytes 393224 | tf_op jit(solution)/shard_map/ppermute | solution.py:22
  56.5 1.3 pad_maximum_fusion.6
  59.8 2.1 %copy.63 = f32[1024,128]{1,0:T(8,128)} copy(f32[1024,128]{0,1:T(8,128)} %get-tuple-element.44) | data formatting | bytes 1048576 | tf_op jit(solution)/shard_map/stack | solution.py:84
  62.1 1.2 copy.66
  63.3 1.9 %constant_dynamic-update-slice_fusion.21 = f32[5,8,128,128]{3,2,0,1:T(8,128)} fusion(f32[5,8,128,128]{3,2,0,1:T(8,128)} %constant_dynamic-update-slice_fusion.22, f32[1,8,128,128]{3,2,0,1:T(8,128)} %bitcast.125), kind=kLoop, calls=%fused_computation.98 | loop fusion | bytes 1048576
  67.8 5.6 %fusion.15 = f32[8,128,128]{2,1,0:T(8,128)S(1)} fusion(f32[5,8,128,128]{3,2,0,1:T(8,128)} %constant_dynamic-update-slice_fusion.18, f32[8,5,128]{2,1,0:T(8,128)S(1)} %copy.8, f32[8,128]{1,0:T(8,128)S(1)} %bitcast.154, f32[8,5,128]{2,1,0:T(8,128)S(1)} %copy.7, f32[8,128]{1,0:T(8,128)S(1)} %bitcast.148), kind=kOutput, calls=%fused_computation.18 | convolution fusion | flops 1014628352 | bytes 3194880 | tf_op jit(solution)/shard_map/bkij,kbjp->bip/dot_general | solution.py:88
  73.8 1.3 collective-permute-start.9
  75.1 7.1 %collective-permute-start.8 = (f32[256,128]{0,1:T(8,128)S(1)}, f32[256,128]{0,1:T(8,128)S(1)}, u32[]{:S(2)}, u32[]{:S(2)}) collective-permute-start(f32[256,128]{0,1:T(8,128)S(1)} %get-tuple-element.42), channel_id=1, source_target_pairs={{0,1},{1,2},{2,3},{3,4},{4,5},{5,6},{6,7},{7,8},{8,9},{9,10},{10,1... | collective-permute-start | bytes 393224 | tf_op jit(solution)/shard_map/ppermute | solution.py:22
  83.0 1.3 pad_maximum_fusion.4
  86.3 2.1 %copy.69 = f32[1024,128]{1,0:T(8,128)} copy(f32[1024,128]{0,1:T(8,128)} %get-tuple-element.40) | data formatting | bytes 1048576 | tf_op jit(solution)/shard_map/stack | solution.py:84
  89.8 1.9 %constant_dynamic-update-slice_fusion.26 = f32[5,8,128,128]{3,2,0,1:T(8,128)} fusion(f32[5,8,128,128]{3,2,0,1:T(8,128)} %constant_dynamic-update-slice_fusion.27, f32[1,8,128,128]{3,2,0,1:T(8,128)} %bitcast.126), kind=kLoop, calls=%fused_computation.103 | loop fusion | bytes 1048576
  94.2 5.6 %fusion.14 = f32[8,128,128]{2,1,0:T(8,128)S(1)} fusion(f32[5,8,128,128]{3,2,0,1:T(8,128)} %constant_dynamic-update-slice_fusion.23, f32[8,5,128]{2,1,0:T(8,128)S(1)} %copy.8, f32[8,128]{1,0:T(8,128)S(1)} %bitcast.155, f32[8,5,128]{2,1,0:T(8,128)S(1)} %copy.7, f32[8,128]{1,0:T(8,128)S(1)} %bitcast.149), kind=kOutput, calls=%fused_computation.17 | convolution fusion | flops 1014628352 | bytes 3194880 | tf_op jit(solution)/shard_map/bkij,kbjp->bip/dot_general | solution.py:88
  100.3 1.3 collective-permute-start.11
  101.6 6.8 %collective-permute-start.10 = (f32[256,128]{0,1:T(8,128)S(1)}, f32[256,128]{0,1:T(8,128)S(1)}, u32[]{:S(2)}, u32[]{:S(2)}) collective-permute-start(f32[256,128]{0,1:T(8,128)S(1)} %get-tuple-element.38), channel_id=1, source_target_pairs={{0,1},{1,2},{2,3},{3,4},{4,5},{5,6},{6,7},{7,8},{8,9},{9,10},{10,1... | collective-permute-start | bytes 393224 | tf_op jit(solution)/shard_map/ppermute | solution.py:22
  109.4 1.3 pad_maximum_fusion.2
  112.7 2.1 %copy.75 = f32[1024,128]{1,0:T(8,128)} copy(f32[1024,128]{0,1:T(8,128)} %get-tuple-element.36) | data formatting | bytes 1048576 | tf_op jit(solution)/shard_map/stack | solution.py:84
  116.2 1.9 %constant_dynamic-update-slice_fusion.31 = f32[5,8,128,128]{3,2,0,1:T(8,128)} fusion(f32[5,8,128,128]{3,2,0,1:T(8,128)} %constant_dynamic-update-slice_fusion.32, f32[1,8,128,128]{3,2,0,1:T(8,128)} %bitcast.127), kind=kLoop, calls=%fused_computation.108 | loop fusion | bytes 1048576
  120.6 5.6 %fusion.13 = f32[8,128,128]{2,1,0:T(8,128)S(1)} fusion(f32[5,8,128,128]{3,2,0,1:T(8,128)} %constant_dynamic-update-slice_fusion.28, f32[8,5,128]{2,1,0:T(8,128)S(1)} %copy.8, f32[8,128]{1,0:T(8,128)S(1)} %bitcast.156, f32[8,5,128]{2,1,0:T(8,128)S(1)} %copy.7, f32[8,128]{1,0:T(8,128)S(1)} %bitcast.150), kind=kOutput, calls=%fused_computation.16 | convolution fusion | flops 1014628352 | bytes 3194880 | tf_op jit(solution)/shard_map/bkij,kbjp->bip/dot_general | solution.py:88
  126.7 1.3 collective-permute-start.13
  128.0 7.1 %collective-permute-start.12 = (f32[256,128]{0,1:T(8,128)S(1)}, f32[256,128]{0,1:T(8,128)S(1)}, u32[]{:S(2)}, u32[]{:S(2)}) collective-permute-start(f32[256,128]{0,1:T(8,128)S(1)} %get-tuple-element.34), channel_id=1, source_target_pairs={{0,1},{1,2},{2,3},{3,4},{4,5},{5,6},{6,7},{7,8},{8,9},{9,10},{10,1... | collective-permute-start | bytes 393224 | tf_op jit(solution)/shard_map/ppermute | solution.py:22
  144.3 5.6 %fusion = f32[8,128,128,1]{2,1,3,0:T(8,128)S(1)} fusion(f32[5,8,128,128]{3,2,0,1:T(8,128)} %constant_dynamic-update-slice_fusion.33, f32[8,5,128]{2,1,0:T(8,128)S(1)} %copy.8, f32[8,128]{1,0:T(8,128)S(1)} %bitcast.157, f32[8,5,128]{2,1,0:T(8,128)S(1)} %copy.7, f32[8,128]{1,0:T(8,128)S(1)} %bitcast.151), kind=kOutput, calls=%fused_computation.1 | convolution fusion | flops 1014497280 | bytes 3194880 | tf_op jit(solution)/shard_map/bkij,kbjp->bip/dot_general | solution.py:88
  150.4 35.0 %all-reduce = (f32[128]{0:T(128)S(1)}, f32[]{:T(128)}) all-reduce(f32[128]{0:T(128)S(1)} %fusion.62, f32[]{:T(128)} %convert_reduce_fusion), channel_id=1, replica_groups=mesh['sections'=2,'tx'=16] {'tx'}, use_global_device_ids=true, to_apply=%region_3.0 | all-reduce | flops 129 | bytes 1032 | tf_op jit(solution)/shard_map/psum | solution.py:113
  (118 shorter events, 51.5 us)
Async XLA Ops:
  0.0 26.0 %copy-start = (f32[1024,128]{1,0:T(8,128)S(1)}, f32[1024,128]{1,0:T(8,128)}, u32[]{:S(2)}) copy-start(f32[1024,128]{1,0:T(8,128)} %param.8) | copy-start | bytes 1572868
  0.8 13.9 %collective-permute-start.3 = (f32[256,128]{0,1:T(8,128)S(1)}, f32[256,128]{0,1:T(8,128)S(1)}, u32[]{:S(2)}, u32[]{:S(2)}) collective-permute-start(f32[256,128]{0,1:T(8,128)S(1)} %mul.55), channel_id=1, source_target_pairs={{1,0},{2,1},{3,2},{4,3},{5,4},{6,5},{7,6},{8,7},{9,8},{10,9},{11,1... | collective-permute-start | bytes 393224 | tf_op jit(solution)/shard_map/ppermute | solution.py:23
  2.1 12.6 %collective-permute-start.2 = (f32[256,128]{0,1:T(8,128)S(1)}, f32[256,128]{0,1:T(8,128)S(1)}, u32[]{:S(2)}, u32[]{:S(2)}) collective-permute-start(f32[256,128]{0,1:T(8,128)S(1)} %mul.54), channel_id=1, source_target_pairs={{0,1},{1,2},{2,3},{3,4},{4,5},{5,6},{6,7},{7,8},{8,9},{9,10},{10,1... | collective-permute-start | bytes 393224 | tf_op jit(solution)/shard_map/ppermute | solution.py:22
  5.9 7.3 %collective-permute-start = (f32[2,256]{1,0:T(2,128)S(1)}, f32[2,256]{1,0:T(2,128)S(1)}, u32[]{:S(2)}, u32[]{:S(2)}) collective-permute-start(f32[2,256]{1,0:T(2,128)S(1)} %get-tuple-element.58), channel_id=1, source_target_pairs={{0,1},{1,2},{2,3},{3,4},{4,5},{5,6},{6,7},{7,8},{8,9},{9,10},{10,1... | collective-permute-start | bytes 6152 | tf_op jit(solution)/shard_map/ppermute | solution.py:22
  10.4 4.3 %collective-permute-start.1 = (f32[2,256]{1,0:T(2,128)S(1)}, f32[2,256]{1,0:T(2,128)S(1)}, u32[]{:S(2)}, u32[]{:S(2)}) collective-permute-start(f32[2,256]{1,0:T(2,128)S(1)} %get-tuple-element.57), channel_id=1, source_target_pairs={{1,0},{2,1},{3,2},{4,3},{5,4},{6,5},{7,6},{8,7},{9,8},{10,9},{11,1... | collective-permute-start | bytes 6152 | tf_op jit(solution)/shard_map/ppermute | solution.py:23
  20.1 5.8 %copy-start.3 = (s32[128]{0:T(128)S(1)}, s32[128]{0:T(128)}, u32[]{:S(2)}) copy-start(s32[128]{0:T(128)} %param.10) | copy-start | bytes 1540
  26.6 5.6 %collective-permute-start.5 = (f32[256,128]{0,1:T(8,128)S(1)}, f32[256,128]{0,1:T(8,128)S(1)}, u32[]{:S(2)}, u32[]{:S(2)}) collective-permute-start(f32[256,128]{0,1:T(8,128)S(1)} %get-tuple-element.49), channel_id=1, source_target_pairs={{1,0},{2,1},{3,2},{4,3},{5,4},{6,5},{7,6},{8,7},{9,8},{10,9},{11,1... | collective-permute-start | bytes 393224 | tf_op jit(solution)/shard_map/ppermute | solution.py:23
  27.9 4.9 %collective-permute-start.4 = (f32[256,128]{0,1:T(8,128)S(1)}, f32[256,128]{0,1:T(8,128)S(1)}, u32[]{:S(2)}, u32[]{:S(2)}) collective-permute-start(f32[256,128]{0,1:T(8,128)S(1)} %get-tuple-element.50), channel_id=1, source_target_pairs={{0,1},{1,2},{2,3},{3,4},{4,5},{5,6},{6,7},{7,8},{8,9},{9,10},{10,1... | collective-permute-start | bytes 393224 | tf_op jit(solution)/shard_map/ppermute | solution.py:22
  41.1 5.9 %copy-start.1 = (f32[1024,128]{1,0:T(8,128)S(1)}, f32[1024,128]{1,0:T(8,128)}, u32[]{:S(2)}) copy-start(f32[1024,128]{1,0:T(8,128)} %param.9) | copy-start | bytes 1572868
  41.1 5.9 %copy-start.4 = (s32[128]{0:T(128)S(1)}, s32[128]{0:T(128)}, u32[]{:S(2)}) copy-start(s32[128]{0:T(128)} %param.11) | copy-start | bytes 1540
  47.6 8.1 %collective-permute-start.7 = (f32[256,128]{0,1:T(8,128)S(1)}, f32[256,128]{0,1:T(8,128)S(1)}, u32[]{:S(2)}, u32[]{:S(2)}) collective-permute-start(f32[256,128]{0,1:T(8,128)S(1)} %get-tuple-element.45), channel_id=1, source_target_pairs={{1,0},{2,1},{3,2},{4,3},{5,4},{6,5},{7,6},{8,7},{9,8},{10,9},{11,1... | collective-permute-start | bytes 393224 | tf_op jit(solution)/shard_map/ppermute | solution.py:23
  48.9 7.6 %collective-permute-start.6 = (f32[256,128]{0,1:T(8,128)S(1)}, f32[256,128]{0,1:T(8,128)S(1)}, u32[]{:S(2)}, u32[]{:S(2)}) collective-permute-start(f32[256,128]{0,1:T(8,128)S(1)} %get-tuple-element.46), channel_id=1, source_target_pairs={{0,1},{1,2},{2,3},{3,4},{4,5},{5,6},{6,7},{7,8},{8,9},{9,10},{10,1... | collective-permute-start | bytes 393224 | tf_op jit(solution)/shard_map/ppermute | solution.py:22
  73.8 8.6 %collective-permute-start.9 = (f32[256,128]{0,1:T(8,128)S(1)}, f32[256,128]{0,1:T(8,128)S(1)}, u32[]{:S(2)}, u32[]{:S(2)}) collective-permute-start(f32[256,128]{0,1:T(8,128)S(1)} %get-tuple-element.41), channel_id=1, source_target_pairs={{1,0},{2,1},{3,2},{4,3},{5,4},{6,5},{7,6},{8,7},{9,8},{10,9},{11,1... | collective-permute-start | bytes 393224 | tf_op jit(solution)/shard_map/ppermute | solution.py:23
  75.1 7.9 %collective-permute-start.8 = (f32[256,128]{0,1:T(8,128)S(1)}, f32[256,128]{0,1:T(8,128)S(1)}, u32[]{:S(2)}, u32[]{:S(2)}) collective-permute-start(f32[256,128]{0,1:T(8,128)S(1)} %get-tuple-element.42), channel_id=1, source_target_pairs={{0,1},{1,2},{2,3},{3,4},{4,5},{5,6},{6,7},{7,8},{8,9},{9,10},{10,1... | collective-permute-start | bytes 393224 | tf_op jit(solution)/shard_map/ppermute | solution.py:22
  100.3 8.4 %collective-permute-start.11 = (f32[256,128]{0,1:T(8,128)S(1)}, f32[256,128]{0,1:T(8,128)S(1)}, u32[]{:S(2)}, u32[]{:S(2)}) collective-permute-start(f32[256,128]{0,1:T(8,128)S(1)} %get-tuple-element.37), channel_id=1, source_target_pairs={{1,0},{2,1},{3,2},{4,3},{5,4},{6,5},{7,6},{8,7},{9,8},{10,9},{11,1... | collective-permute-start | bytes 393224 | tf_op jit(solution)/shard_map/ppermute | solution.py:23
  101.6 7.8 %collective-permute-start.10 = (f32[256,128]{0,1:T(8,128)S(1)}, f32[256,128]{0,1:T(8,128)S(1)}, u32[]{:S(2)}, u32[]{:S(2)}) collective-permute-start(f32[256,128]{0,1:T(8,128)S(1)} %get-tuple-element.38), channel_id=1, source_target_pairs={{0,1},{1,2},{2,3},{3,4},{4,5},{5,6},{6,7},{7,8},{8,9},{9,10},{10,1... | collective-permute-start | bytes 393224 | tf_op jit(solution)/shard_map/ppermute | solution.py:22
  126.3 8.8 %copy-start.2 = (s32[8]{0:T(128)S(1)}, s32[8]{0:T(128)}, u32[]{:S(2)}) copy-start(s32[8]{0:T(128)} %param.7) | copy-start | bytes 100
  126.7 9.3 %collective-permute-start.13 = (f32[256,128]{0,1:T(8,128)S(1)}, f32[256,128]{0,1:T(8,128)S(1)}, u32[]{:S(2)}, u32[]{:S(2)}) collective-permute-start(f32[256,128]{0,1:T(8,128)S(1)} %get-tuple-element.33), channel_id=1, source_target_pairs={{1,0},{2,1},{3,2},{4,3},{5,4},{6,5},{7,6},{8,7},{9,8},{10,9},{11,1... | collective-permute-start | bytes 393224 | tf_op jit(solution)/shard_map/ppermute | solution.py:23
  128.0 8.0 %collective-permute-start.12 = (f32[256,128]{0,1:T(8,128)S(1)}, f32[256,128]{0,1:T(8,128)S(1)}, u32[]{:S(2)}, u32[]{:S(2)}) collective-permute-start(f32[256,128]{0,1:T(8,128)S(1)} %get-tuple-element.34), channel_id=1, source_target_pairs={{0,1},{1,2},{2,3},{3,4},{4,5},{5,6},{6,7},{7,8},{8,9},{9,10},{10,1... | collective-permute-start | bytes 393224 | tf_op jit(solution)/shard_map/ppermute | solution.py:22
where the time goes:
time: 189 us; the launch traced here: 187 us
  local copies, waits for them, and re-layouts  55.6 us (29%)
  starting transfers between devices  48.4 us (26%)
  blocking collectives  35 us (19%)
  matrix products  34.9 us (18%)
  other arithmetic  10.1 us (5%)
  waiting for transfers between devices  2.64 us (1%)
    ppermute x7, starting transfers between devices, extended_2(): before = lax.ppermute(last, axis, up)  39.3 us
    psum x1, blocking collectives, body(): lax.psum((jnp.sum(flux_out, axis=0), jnp.sum(counts.astype(jnp.float32)))...  35 us
    dot_general x6, matrix products, apply_tiles(): jnp.einsum('bkij,kbjp->bip', band_tiles, val_win, precision=lax.Precision...  33.7 us
    another operation x35, local copies, waits for them, and re-layouts, apply_tiles(): jnp.stack([values_ext[slot_k * BLK:slot_k * BLK + cells_dev] for slot_k i...  26.6 us
    unnamed x40, local copies, waits for them, and re-layouts  25.1 us
    ppermute x7, starting transfers between devices, extended_2(): after = lax.ppermute(first, axis, down)  9.04 us
    concatenate x6, other arithmetic, extended_2(): x = jnp.concatenate([before, x, after], axis=dim)  6.21 us
  transfers between devices with their start and end apart: 14, of which 4 were waited for; matrix products, arithmetic and copies ran while one was open for 3% of the time, Pallas kernels for 0%

commit v1 on v0

v1 whole, which is shorter than its diff:
```python
import functools
import math

import jax
import jax.numpy as jnp
from jax import lax
from jax.experimental import pallas as pl
from jax.experimental.pallas import tpu as pltpu
from jax.sharding import PartitionSpec as P

BLK = 128
HB = 2
ITERS = 3
RIM = HB * BLK
FAR = 1.0e6

entropy = 0.5
relaxation = 1.0
FACTOR = relaxation / (relaxation + entropy)
LOG2E = math.log2(math.e)
POWER = FACTOR * LOG2E
ROUNDS = 2 * ITERS - 1
SETS = 2


def split(x):
    hi = x.astype(jnp.bfloat16)
    lo = (x - hi.astype(jnp.float32)).astype(jnp.bfloat16)
    return hi, lo


def kernel(
    n,
    pos_ref,
    counts_ref,
    lig_of_ref,
    rec_of_ref,
    lig_hbm,
    rec_hbm,
    flux_hbm,
    scale_ref,
    lig,
    rec,
    own,
    rows,
    pos_send,
    pos_recv,
    xj,
    yj,
    live,
    k_hi,
    k_lo,
    logs,
    values,
    send,
    recv,
    flux_t,
    flux,
    sums,
    in_sem,
    out_sem,
    pos_send_sem,
    pos_recv_sem,
    send_sem,
    recv_sem,
    sum_send_sem,
    sum_recv_sem,
):
    cells = pos_ref.shape[1]
    nblock = cells // BLK
    tiles = cells // RIM
    half = logs.shape[1] // SETS
    me = lax.axis_index("tx")
    has = (me > 0, me < n - 1)
    beside = (lax.rem(me + n - 1, n), lax.rem(me + 1, n))

    lig_copy = pltpu.make_async_copy(lig_hbm, lig, in_sem.at[0])
    rec_copy = pltpu.make_async_copy(rec_hbm, rec, in_sem.at[1])
    lig_copy.start()
    rec_copy.start()

    barrier = pltpu.get_barrier_semaphore()

    @pl.loop(1, n)
    def _(d):
        pl.semaphore_signal(
            barrier,
            inc=1,
            device_id={"tx": lax.rem(me + d, n)},
            device_id_type=pl.DeviceIdType.MESH,
        )

    def remote(src, dst, ssem, rsem, to):
        return pltpu.make_async_remote_copy(
            src_ref=src,
            dst_ref=dst,
            send_sem=ssem,
            recv_sem=rsem,
            device_id={"tx": to},
            device_id_type=pl.DeviceIdType.MESH,
        )

    lane = lax.broadcasted_iota(jnp.int32, (1, BLK), 1)
    live_count = jnp.zeros((1, BLK), jnp.float32)
    for b in range(nblock):
        count = counts_ref[b]
        mask = lane < count
        live[:, b * BLK : (b + 1) * BLK] = jnp.where(mask, 1.0, 0.0)
        live_count = live_count + count.astype(jnp.float32)
        x = pos_ref[0:1, b * BLK : (b + 1) * BLK] * (1.0 / HB)
        y = pos_ref[1:2, b * BLK : (b + 1) * BLK] * (1.0 / HB)
        own[b, 0:1, :] = x
        own[b, 1:2, :] = y
        rows[b, 0:1, :] = jnp.where(mask, x, FAR)
        rows[b, 1:2, :] = y
    for b in range(HB):
        pos_send[0, b] = rows[b]
        pos_send[1, b] = rows[nblock - HB + b]

    pl.semaphore_wait(barrier, n - 1)

    def pos_copy(side):
        return remote(
            pos_send.at[side],
            pos_recv.at[1 - side],
            pos_send_sem.at[side],
            pos_recv_sem.at[1 - side],
            beside[side],
        )

    def pos_arrival(side):
        return remote(
            pos_send.at[side],
            pos_recv.at[side],
            pos_send_sem.at[side],
            pos_recv_sem.at[side],
            beside[side],
        )

    for side in range(2):
        pl.when(has[side])(pos_copy(side).start)

    def columns(x_row, y_row, at):
        xj[at : at + BLK, :] = jnp.broadcast_to(x_row, (BLK, BLK)).T
        yj[at : at + BLK, :] = jnp.broadcast_to(y_row, (BLK, BLK)).T

    for b in range(nblock):
        columns(rows[b, 0:1, :], rows[b, 1:2, :], RIM + b * BLK)

    def tile_of(t):
        for q in range(HB):
            xi = own[HB * t + q, 0:1, :]
            yi = own[HB * t + q, 1:2, :]
            for w in range(3 * HB):
                at = (pl.ds(w * BLK, BLK), pl.ds(q * BLK, BLK))
                if abs(w - HB - q) > HB:
                    k_hi[t, at[0], at[1]] = jnp.zeros((BLK, BLK), jnp.bfloat16)
                    k_lo[t, at[0], at[1]] = jnp.zeros((BLK, BLK), jnp.bfloat16)
                    continue
                here = pl.ds(pl.multiple_of(t * RIM + w * BLK, BLK), BLK)
                c = jnp.square(xj[here, :] - xi) + jnp.square(yj[here, :] - yi)
                taper = jnp.square(jnp.maximum(1.0 - c, 0.0))
                hi, lo = split(taper * jnp.exp2(c * (-LOG2E / entropy)))
                k_hi[t, at[0], at[1]] = hi
                k_lo[t, at[0], at[1]] = lo

    lax.fori_loop(1, tiles - 1, lambda t, _: (tile_of(t), 0)[1], 0)

    def log_pairs(which, source, of_ref):
        pick = jnp.where(
            lax.broadcasted_iota(jnp.int32, (BLK, BLK), 0) == of_ref[...], 1.0, 0.0
        )
        pick = pick.T.astype(jnp.bfloat16)
        pick2 = jnp.concatenate([pick, pick], axis=1)

        @pl.loop(0, tiles)
        def _(t):
            here = pl.ds(pl.multiple_of(t * RIM, RIM), RIM)
            x = jnp.concatenate(split(source[here, :]), axis=1)
            picked = lax.dot_general(
                pick2, x, (((1,), (1,)), ((), ())), preferred_element_type=jnp.float32
            )
            logs[which, :, here] = POWER * jnp.log(picked)

    lig_copy.wait()
    log_pairs(0, lig, lig_of_ref)

    far = jnp.full((1, BLK), FAR, jnp.float32)
    for side in range(2):
        at = 0 if side == 0 else RIM + cells

        @pl.when(has[side])
        def _():
            pos_arrival(side).wait_recv()
            for b in range(HB):
                columns(
                    pos_recv[side, b, 0:1, :], pos_recv[side, b, 1:2, :], at + b * BLK
                )

        @pl.when(jnp.logical_not(has[side]))
        def _():
            for b in range(HB):
                columns(far, far, at + b * BLK)

    lax.fori_loop(0, 2, lambda i, _: (tile_of(i * (tiles - 1)), 0)[1], 0)

    for parity in range(2):
        for s in range(SETS):
            for at in (0, RIM + cells):
                values[parity, s, :, at : at + RIM] = jnp.zeros(
                    (2 * half, RIM), jnp.bfloat16
                )

    def copy_out(k, s, side):
        return remote(
            send.at[k, s, side],
            recv.at[k, s, 1 - side],
            send_sem.at[k, s, side],
            recv_sem.at[k, s, 1 - side],
            beside[side],
        )

    def arrival(k, s, side):
        return remote(
            send.at[k, s, side],
            recv.at[k, s, side],
            send_sem.at[k, s, side],
            recv_sem.at[k, s, side],
            beside[side],
        )

    def scaled(which, s, t, mass):
        alive = live[:, t * RIM : (t + 1) * RIM]
        log_have = logs[which, s * half : (s + 1) * half, t * RIM : (t + 1) * RIM]
        return alive * jnp.exp2(log_have - POWER * jnp.log(mass + (1.0 - alive)))

    def keep(parity, s, t, w):
        hi, lo = split(w)
        at = RIM * (t + 1)
        values[parity, s, 0:half, at : at + RIM] = hi
        values[parity, s, half:, at : at + RIM] = lo

    edges = ((0, 0), (1, tiles - 1))

    def start(k, s):
        for side, _ in edges:
            pl.when(has[side])(copy_out(k, s, side).start)

    def first(t):
        ones = jnp.ones((16, 3 * RIM), jnp.bfloat16)
        return jnp.dot(ones, k_hi[t], preferred_element_type=jnp.float32)[0:1, :]

    masses = [first(t) for _, t in edges]
    for s in range(SETS):
        for side, t in edges:
            w = scaled(0, s, t, masses[side])
            send[0, s, side] = w
            keep(0, s, t, w)
        start(0, s)
    for t in range(1, tiles - 1):
        mass = first(t)
        for s in range(SETS):
            keep(0, s, t, scaled(0, s, t, mass))

    rec_copy.wait()
    log_pairs(1, rec, rec_of_ref)

    def arrive(k, parity, s):
        for side, _ in edges:
            at = 0 if side == 0 else RIM + cells

            @pl.when(has[side])
            def _():
                arrival(k, s, side).wait_recv()
                hi, lo = split(recv[k, s, side])
                values[parity, s, 0:half, at : at + RIM] = hi
                values[parity, s, half:, at : at + RIM] = lo

    def mass_of(parity, s, t):
        both = jnp.dot(
            values[parity, s, :, t * RIM : (t + 3) * RIM],
            k_hi[t],
            preferred_element_type=jnp.float32,
        )
        return both[0:half] + both[half:]

    def one_round(k, parity):
        which = 1 - parity
        for s in range(SETS):
            arrive(k, parity, s)
            for side, t in edges:
                w = scaled(which, s, t, mass_of(parity, s, t))
                send[k + 1, s, side] = w
                keep(1 - parity, s, t, w)
            start(k + 1, s)
        for s in range(SETS):
            for t in range(1, tiles - 1):
                keep(1 - parity, s, t, scaled(which, s, t, mass_of(parity, s, t)))

    def two_rounds(i, carry):
        one_round(2 * i, 0)
        one_round(2 * i + 1, 1)
        return carry

    lax.fori_loop(0, (ROUNDS - 1) // 2, two_rounds, 0)

    last = ROUNDS - 1
    parity = last % 2

    def finish(s, t):
        gathered = mass_of(parity, s, t) + jnp.dot(
            values[parity, s, 0:half, t * RIM : (t + 3) * RIM],
            k_lo[t],
            preferred_element_type=jnp.float32,
        )
        flux_t[s * half : (s + 1) * half, t * RIM : (t + 1) * RIM] = (
            scaled(1, s, t, gathered) * gathered
        )

    def turn(t):
        total = jnp.zeros((1, BLK), jnp.float32)
        for b in range(HB * t, HB * (t + 1)):
            out = flux_t[:, b * BLK : (b + 1) * BLK].T
            flux[b * BLK : (b + 1) * BLK, :] = out
            total = total + jnp.sum(out, axis=0, keepdims=True)
        return total

    totals = jnp.zeros((1, BLK), jnp.float32)
    for t in range(1, tiles - 1):
        for s in range(SETS):
            finish(s, t)
        totals = totals + turn(t)
    for s in range(SETS):
        arrive(last, parity, s)
        for _, t in edges:
            finish(s, t)
    for _, t in edges:
        totals = totals + turn(t)

    sums[0, 0:1, :] = totals
    sums[0, 1:2, :] = live_count

    def sum_copy(d):
        return remote(
            sums.at[0],
            sums.at[d],
            sum_send_sem.at[d],
            sum_recv_sem.at[d],
            lax.rem(me + d, n),
        )

    @pl.loop(1, n)
    def _(d):
        sum_copy(d).start()

    out_copy = pltpu.make_async_copy(flux, flux_hbm, out_sem)
    out_copy.start()

    for side in range(2):

        @pl.when(has[side])
        def _():
            pos_copy(side).wait_send()
            for s in range(SETS):
                for k in range(ROUNDS):
                    copy_out(k, s, side).wait_send()

    @pl.loop(1, n)
    def _(d):
        sum_copy(d).wait()

    whole = jnp.sum(sums[...], axis=0)
    scale_ref[0:1, :] = whole[1:2, :] / whole[0:1, :]
    out_copy.wait()


def body(positions, counts, ligands, receptors, lig_of_pair, rec_of_pair):
    n = lax.axis_size("tx")
    cells = positions.shape[1]
    nblock = counts.shape[0]
    tiles = cells // RIM
    pairs = lig_of_pair.shape[0]
    wide = cells + 2 * RIM
    half = pairs // SETS
    f32, bf16 = jnp.float32, jnp.bfloat16
    vmem = pl.BlockSpec(memory_space=pltpu.VMEM)
    smem = pl.BlockSpec(memory_space=pltpu.SMEM)
    hbm = pl.BlockSpec(memory_space=pl.ANY)
    flux, scale = pl.pallas_call(
        functools.partial(kernel, n),
        out_shape=(
            jax.ShapeDtypeStruct((cells, pairs), f32),
            jax.ShapeDtypeStruct((1, pairs), f32),
        ),
        in_specs=[vmem, smem, vmem, vmem, hbm, hbm],
        out_specs=(hbm, vmem),
        scratch_shapes=[
            pltpu.VMEM(ligands.shape, f32),
            pltpu.VMEM(receptors.shape, f32),
            pltpu.VMEM((nblock, 8, BLK), f32),
            pltpu.VMEM((nblock, 8, BLK), f32),
            pltpu.VMEM((2, HB, 8, BLK), f32),
            pltpu.VMEM((2, HB, 8, BLK), f32),
            pltpu.VMEM((wide, BLK), f32),
            pltpu.VMEM((wide, BLK), f32),
            pltpu.VMEM((1, cells), f32),
            pltpu.VMEM((tiles, 3 * RIM, RIM), bf16),
            pltpu.VMEM((tiles, 3 * RIM, RIM), bf16),
            pltpu.VMEM((2, pairs, cells), f32),
            pltpu.VMEM((2, SETS, 2 * half, wide), bf16),
            pltpu.VMEM((ROUNDS, SETS, 2, half, RIM), f32),
            pltpu.VMEM((ROUNDS, SETS, 2, half, RIM), f32),
            pltpu.VMEM((pairs, cells), f32),
            pltpu.VMEM((cells, pairs), f32),
            pltpu.VMEM((n, 2, BLK), f32),
            pltpu.SemaphoreType.DMA((2,)),
            pltpu.SemaphoreType.DMA,
            pltpu.SemaphoreType.DMA((2,)),
            pltpu.SemaphoreType.DMA((2,)),
            pltpu.SemaphoreType.DMA((ROUNDS, SETS, 2)),
            pltpu.SemaphoreType.DMA((ROUNDS, SETS, 2)),
            pltpu.SemaphoreType.DMA((n,)),
            pltpu.SemaphoreType.DMA((n,)),
        ],
        compiler_params=pltpu.CompilerParams(
            collective_id=0, has_side_effects=True, vmem_limit_bytes=32 * 1024 * 1024
        ),
    )(
        positions,
        counts,
        lig_of_pair.reshape(1, pairs),
        rec_of_pair.reshape(1, pairs),
        ligands,
        receptors,
    )
    return flux * scale


def solution(mesh):
    in_specs = (
        P(None, ("sections", "tx")),
        P(("sections", "tx")),
        P(("sections", "tx"), None),
        P(("sections", "tx"), None),
        P(),
        P(),
    )
    out_specs = P(("sections", "tx"), None)
    return jax.shard_map(body, mesh=mesh, in_specs=in_specs, out_specs=out_specs, check_vma=False)
```

time: 189 us -> 38.5 us (0.20)
  local copies, waits for them, and re-layouts: 55.6 us -> 3.46 us
  starting transfers between devices: 48.4 us -> 0 us
  blocking collectives: 35 us -> 0 us
  matrix products: 34.9 us -> 0 us
  Pallas kernels: 0 us -> 33.9 us
  other arithmetic: 10.1 us -> 0.83 us
  waiting for transfers between devices: 2.64 us -> 0 us
    ppermute x14 -> x0, starting transfers between devices: 48.4 us -> none  [the longest x7 39.3 us: extended_2(): before = lax.ppermute(last, axis, up)]
    psum x1 -> x0, blocking collectives: 35 us -> none  [body(): lax.psum((jnp.sum(flux_out, axis=0), jnp.sum(counts.astype(jnp.float32)))...]
    dot_general x8 -> x0, matrix products: 34.9 us -> none  [the longest x6 33.7 us: apply_tiles(): jnp.einsum('bkij,kbjp->bip', band_tiles, val_win, precision=lax.Precision...]
    pallas_call x0 -> x1, Pallas kernels: none -> 33.9 us  [body(): pl.pallas_call(functools.partial(kernel, n), out_shape=(jax.ShapeDtypeStr...]
    another operation x36 -> x0, local copies, waits for them, and re-layouts: 26.6 us -> none  [the longest x35 26.6 us: apply_tiles(): jnp.stack([values_ext[slot_k * BLK:slot_k * BLK + cells_dev] for slot_k i...]
    unnamed x40 -> x12, local copies, waits for them, and re-layouts: 25.1 us -> 3.46 us
    concatenate x6 -> x0, other arithmetic: 6.21 us -> none  [extended_2(): x = jnp.concatenate([before, x, after], axis=dim)]
    ppermute x14 -> x0, waiting for transfers between devices: 2.64 us -> none  [the longest x7 2.62 us: extended_2(): before = lax.ppermute(last, axis, up)]
  transfers between devices with their start and end apart: 14 -> 0, of which waited for: 4 -> 0; matrix products, arithmetic and copies ran while one was open for 3% -> 0% of each run, Pallas kernels for 0% -> 0%
where the time goes in v1:
time: 38.5 us; the launch traced here: 38.2 us
  Pallas kernels  33.9 us (88%)
  local copies, waits for them, and re-layouts  3.46 us (9%)
  other arithmetic  0.83 us (2%)
    pallas_call x1, Pallas kernels, body(): pl.pallas_call(functools.partial(kernel, n), out_shape=(jax.ShapeDtypeStr...  33.9 us
    unnamed x12, local copies, waits for them, and re-layouts  3.46 us
    mul x1, other arithmetic, body(): return flux * scale  0.83 us

profile of v1, /device:TPU:0, one launch (start us, length us, event | category | flops | bytes accessed | tf_op | source)
XLA Modules:
  0.0 38.2 jit_solution(18008061331075514272)
XLA Ops:
  0.0 0.0 copy-start.3
  0.0 0.0 copy-start.4
  0.0 0.0 copy-start.5
  0.0 0.6 %copy-done.3 = s32[8]{0:T(128)S(1)} copy-done((s32[8]{0:T(128)S(1)}, s32[8]{0:T(128)}, u32[]{:S(2)}) %copy-start.3) | copy-done | bytes 56
  0.7 0.0 copy-done.4
  0.7 0.0 copy-done.5
  0.7 0.0 copy-start
  0.7 1.0 %copy-done = f32[1024,128]{1,0:T(8,128)S(1)} copy-done((f32[1024,128]{1,0:T(8,128)S(1)}, f32[1024,128]{1,0:T(8,128)}, u32[]{:S(2)}) %copy-start) | copy-done | bytes 524312
  1.7 0.0 copy-start.1
  1.7 1.0 %copy-done.1 = f32[1024,128]{1,0:T(8,128)S(1)} copy-done((f32[1024,128]{1,0:T(8,128)S(1)}, f32[1024,128]{1,0:T(8,128)}, u32[]{:S(2)}) %copy-start.1) | copy-done | bytes 524312
  2.8 0.0 copy-start.2
  2.8 0.7 %copy-done.2 = f32[2,1024]{1,0:T(2,128)S(1)} copy-done((f32[2,1024]{1,0:T(2,128)S(1)}, f32[2,1024]{1,0:T(2,128)}, u32[]{:S(2)}) %copy-start.2) | copy-done | bytes 8216
  3.5 33.9 %shard_map.64 = (f32[1024,128]{1,0:T(8,128)S(1)}, f32[1,128]{1,0:T(1,128)S(1)}) custom-call(f32[2,1024]{1,0:T(2,128)S(1)} %copy-done.2, s32[8]{0:T(128)S(1)} %copy-done.3, s32[1,128]{1,0:T(1,128)S(1)} %bitcast.3, s32[1,128]{1,0:T(1,128)S(1)} %bitcast.4, f32[1024,128]{1,0:T(8,128)S(1)} %copy-done, f32[1024,128]{1,0:T(8,128)S(1)} %copy-done.1), custom_call_target="tpu_custom_call" | custom-call | tf_op jit(solution)/shard_map/pallas_call | solution.py:389
  37.4 0.8 %broadcast_multiply_fusion = f32[1024,128]{1,0:T(8,128)} fusion(f32[1024,128]{1,0:T(8,128)S(1)} %get-tuple-element.7, f32[128]{0:T(128)S(1)} %bitcast.5), kind=kLoop, calls=%fused_computation | loop fusion | flops 131072 | bytes 1049088 | tf_op jit(solution)/shard_map/mul | solution.py:436
Async XLA Ops:
  0.0 0.7 %copy-start.3 = (s32[8]{0:T(128)S(1)}, s32[8]{0:T(128)}, u32[]{:S(2)}) copy-start(s32[8]{0:T(128)} %counts_ref.1) | copy-start | bytes 100
  0.0 0.7 %copy-start.4 = (s32[128]{0:T(128)S(1)}, s32[128]{0:T(128)}, u32[]{:S(2)}) copy-start(s32[128]{0:T(128)} %param.10) | copy-start | bytes 1540
  0.0 0.7 %copy-start.5 = (s32[128]{0:T(128)S(1)}, s32[128]{0:T(128)}, u32[]{:S(2)}) copy-start(s32[128]{0:T(128)} %param.11) | copy-start | bytes 1540
  0.7 1.0 %copy-start = (f32[1024,128]{1,0:T(8,128)S(1)}, f32[1024,128]{1,0:T(8,128)}, u32[]{:S(2)}) copy-start(f32[1024,128]{1,0:T(8,128)} %lig_hbm.1) | copy-start | bytes 1572868
  1.7 1.0 %copy-start.1 = (f32[1024,128]{1,0:T(8,128)S(1)}, f32[1024,128]{1,0:T(8,128)}, u32[]{:S(2)}) copy-start(f32[1024,128]{1,0:T(8,128)} %rec_hbm.1) | copy-start | bytes 1572868
  2.8 0.7 %copy-start.2 = (f32[2,1024]{1,0:T(2,128)S(1)}, f32[2,1024]{1,0:T(2,128)}, u32[]{:S(2)}) copy-start(f32[2,1024]{1,0:T(2,128)} %pos_ref.1) | copy-start | bytes 24580

commit v2 on v1

--- a/solution.py
+++ b/solution.py
@@ -31,14 +31,18 @@
 
 def kernel(
     n,
+    pos_hbm,
+    counts_hbm,
+    lig_of_hbm,
+    rec_of_hbm,
+    lig_hbm,
+    rec_hbm,
+    flux_hbm,
+    scale_ref,
     pos_ref,
     counts_ref,
     lig_of_ref,
     rec_of_ref,
-    lig_hbm,
-    rec_hbm,
-    flux_hbm,
-    scale_ref,
     lig,
     rec,
     own,
@@ -66,7 +70,7 @@
     sum_send_sem,
     sum_recv_sem,
 ):
-    cells = pos_ref.shape[1]
+    cells = pos_hbm.shape[1]
     nblock = cells // BLK
     tiles = cells // RIM
     half = logs.shape[1] // SETS
@@ -74,8 +78,16 @@
     has = (me > 0, me < n - 1)
     beside = (lax.rem(me + n - 1, n), lax.rem(me + 1, n))
 
-    lig_copy = pltpu.make_async_copy(lig_hbm, lig, in_sem.at[0])
-    rec_copy = pltpu.make_async_copy(rec_hbm, rec, in_sem.at[1])
+    counts_copy = pltpu.make_async_copy(counts_hbm, counts_ref, in_sem.at[0])
+    pos_copy_in = pltpu.make_async_copy(pos_hbm, pos_ref, in_sem.at[1])
+    lig_of_copy = pltpu.make_async_copy(lig_of_hbm, lig_of_ref, in_sem.at[2])
+    rec_of_copy = pltpu.make_async_copy(rec_of_hbm, rec_of_ref, in_sem.at[3])
+    lig_copy = pltpu.make_async_copy(lig_hbm, lig, in_sem.at[4])
+    rec_copy = pltpu.make_async_copy(rec_hbm, rec, in_sem.at[5])
+    counts_copy.start()
+    pos_copy_in.start()
+    lig_of_copy.start()
+    rec_of_copy.start()
     lig_copy.start()
     rec_copy.start()
 
@@ -100,6 +112,8 @@
             device_id_type=pl.DeviceIdType.MESH,
         )
 
+    counts_copy.wait()
+    pos_copy_in.wait()
     lane = lax.broadcasted_iota(jnp.int32, (1, BLK), 1)
     live_count = jnp.zeros((1, BLK), jnp.float32)
     for b in range(nblock):
@@ -182,6 +196,7 @@
             )
             logs[which, :, here] = POWER * jnp.log(picked)
 
+    lig_of_copy.wait()
     lig_copy.wait()
     log_pairs(0, lig, lig_of_ref)
 
@@ -262,6 +277,7 @@
         for s in range(SETS):
             keep(0, s, t, scaled(0, s, t, mass))
 
+    rec_of_copy.wait()
     rec_copy.wait()
     log_pairs(1, rec, rec_of_ref)
 
@@ -385,16 +401,20 @@
     f32, bf16 = jnp.float32, jnp.bfloat16
     vmem = pl.BlockSpec(memory_space=pltpu.VMEM)
     smem = pl.BlockSpec(memory_space=pltpu.SMEM)
-    hbm = pl.BlockSpec(memory_space=pl.ANY)
+    hbm = pl.BlockSpec(memory_space=pltpu.HBM)
     flux, scale = pl.pallas_call(
         functools.partial(kernel, n),
         out_shape=(
             jax.ShapeDtypeStruct((cells, pairs), f32),
             jax.ShapeDtypeStruct((1, pairs), f32),
         ),
-        in_specs=[vmem, smem, vmem, vmem, hbm, hbm],
+        in_specs=[hbm] * 6,
         out_specs=(hbm, vmem),
         scratch_shapes=[
+            pltpu.VMEM(positions.shape, f32),
+            pltpu.SMEM(counts.shape, jnp.int32),
+            pltpu.VMEM((1, pairs), jnp.int32),
+            pltpu.VMEM((1, pairs), jnp.int32),
             pltpu.VMEM(ligands.shape, f32),
             pltpu.VMEM(receptors.shape, f32),
             pltpu.VMEM((nblock, 8, BLK), f32),
@@ -413,7 +433,7 @@
             pltpu.VMEM((pairs, cells), f32),
             pltpu.VMEM((cells, pairs), f32),
             pltpu.VMEM((n, 2, BLK), f32),
-            pltpu.SemaphoreType.DMA((2,)),
+            pltpu.SemaphoreType.DMA((6,)),
             pltpu.SemaphoreType.DMA,
             pltpu.SemaphoreType.DMA((2,)),
             pltpu.SemaphoreType.DMA((2,)),
@@ -423,7 +443,7 @@
             pltpu.SemaphoreType.DMA((n,)),
         ],
         compiler_params=pltpu.CompilerParams(
-            collective_id=0, has_side_effects=True, vmem_limit_bytes=32 * 1024 * 1024
+            collective_id=0, has_side_effects=True
         ),
     )(
         positions,

time: 38.5 us -> 36.6 us (0.951)
  local copies, waits for them, and re-layouts: 3.46 us -> 0.66 us
  other arithmetic: 0.83 us -> 1.87 us
    unnamed x12 -> x2, local copies, waits for them, and re-layouts: 3.46 us -> 0.66 us
    mul x1, other arithmetic: 0.83 us -> 1.87 us  [body(): return flux * scale]
where the time goes in v2:
time: 36.6 us; the launch traced here: 36.4 us
  Pallas kernels  33.8 us (92%)
  other arithmetic  1.87 us (5%)
  local copies, waits for them, and re-layouts  0.66 us (2%)
    pallas_call x1, Pallas kernels, body(): pl.pallas_call(functools.partial(kernel, n), out_shape=(jax.ShapeDtypeStr...  33.8 us
    mul x1, other arithmetic, body(): return flux * scale  1.87 us

profile of v2, /device:TPU:0, one launch (start us, length us, event | category | flops | bytes accessed | tf_op | source)
XLA Modules:
  0.0 36.4 jit_solution(12438417495352766615)
XLA Ops:
  0.0 33.8 %shard_map.64 = (f32[1024,128]{1,0:T(8,128)}, f32[1,128]{1,0:T(1,128)}) custom-call(f32[2,1024]{1,0:T(2,128)} %pos_hbm.1, s32[8]{0:T(128)} %counts_hbm.1, s32[1,128]{1,0:T(1,128)} %bitcast.3, s32[1,128]{1,0:T(1,128)} %bitcast.4, f32[1024,128]{1,0:T(8,128)} %lig_hbm.1, f32[1024,128]{1,0:T(8,128)} %rec_hbm.1), custom_call_target="tpu_custom_call" | custom-call | tf_op jit(solution)/shard_map/pallas_call | solution.py:405
  33.8 0.0 copy-start
  33.9 0.7 %copy-done = f32[1,128]{1,0:T(1,128)S(1)} copy-done((f32[1,128]{1,0:T(1,128)S(1)}, f32[1,128]{1,0:T(1,128)}, u32[]{:S(2)}) %copy-start) | copy-done | bytes 536
  34.5 1.9 %broadcast_multiply_fusion = f32[1024,128]{1,0:T(8,128)} fusion(f32[1024,128]{1,0:T(8,128)} %get-tuple-element.7, f32[128]{0:T(128)S(1)} %bitcast.5), kind=kLoop, calls=%fused_computation | loop fusion | flops 131072 | bytes 1049088 | tf_op jit(solution)/shard_map/mul | solution.py:456
Async XLA Ops:
  33.8 0.7 %copy-start = (f32[1,128]{1,0:T(1,128)S(1)}, f32[1,128]{1,0:T(1,128)}, u32[]{:S(2)}) copy-start(f32[1,128]{1,0:T(1,128)} %get-tuple-element.8) | copy-start | bytes 1540

commit v3 on v2

--- a/solution.py
+++ b/solution.py
@@ -19,7 +19,9 @@
 FACTOR = relaxation / (relaxation + entropy)
 LOG2E = math.log2(math.e)
 POWER = FACTOR * LOG2E
-ROUNDS = 2 * ITERS - 1
+ROUNDS = ITERS - 1
+REACH = 2 * HB
+WIDE = REACH * BLK
 SETS = 2
 
 
@@ -65,6 +67,8 @@
     out_sem,
     pos_send_sem,
     pos_recv_sem,
+    lig_send_sem,
+    lig_recv_sem,
     send_sem,
     recv_sem,
     sum_send_sem,
@@ -82,7 +86,9 @@
     pos_copy_in = pltpu.make_async_copy(pos_hbm, pos_ref, in_sem.at[1])
     lig_of_copy = pltpu.make_async_copy(lig_of_hbm, lig_of_ref, in_sem.at[2])
     rec_of_copy = pltpu.make_async_copy(rec_of_hbm, rec_of_ref, in_sem.at[3])
-    lig_copy = pltpu.make_async_copy(lig_hbm, lig, in_sem.at[4])
+    lig_copy = pltpu.make_async_copy(
+        lig_hbm, lig.at[pl.ds(RIM, cells)], in_sem.at[4]
+    )
     rec_copy = pltpu.make_async_copy(rec_hbm, rec, in_sem.at[5])
     counts_copy.start()
     pos_copy_in.start()
@@ -119,17 +125,17 @@
     for b in range(nblock):
         count = counts_ref[b]
         mask = lane < count
-        live[:, b * BLK : (b + 1) * BLK] = jnp.where(mask, 1.0, 0.0)
+        live[:, RIM + b * BLK : RIM + (b + 1) * BLK] = jnp.where(mask, 1.0, 0.0)
         live_count = live_count + count.astype(jnp.float32)
         x = pos_ref[0:1, b * BLK : (b + 1) * BLK] * (1.0 / HB)
         y = pos_ref[1:2, b * BLK : (b + 1) * BLK] * (1.0 / HB)
-        own[b, 0:1, :] = x
-        own[b, 1:2, :] = y
+        own[HB + b, 0:1, :] = x
+        own[HB + b, 1:2, :] = y
         rows[b, 0:1, :] = jnp.where(mask, x, FAR)
         rows[b, 1:2, :] = y
-    for b in range(HB):
+    for b in range(REACH):
         pos_send[0, b] = rows[b]
-        pos_send[1, b] = rows[nblock - HB + b]
+        pos_send[1, b] = rows[nblock - REACH + b]
 
     pl.semaphore_wait(barrier, n - 1)
 
@@ -151,15 +157,37 @@
             beside[side],
         )
 
+    ends = (0, RIM + cells)
+
+    def lig_out(side):
+        return remote(
+            lig_hbm.at[pl.ds(0 if side == 0 else cells - RIM, RIM)],
+            lig.at[pl.ds(ends[1 - side], RIM)],
+            lig_send_sem.at[side],
+            lig_recv_sem.at[1 - side],
+            beside[side],
+        )
+
+    def lig_arrival(side):
+        return remote(
+            lig_hbm.at[pl.ds(0 if side == 0 else cells - RIM, RIM)],
+            lig.at[pl.ds(ends[side], RIM)],
+            lig_send_sem.at[side],
+            lig_recv_sem.at[side],
+            beside[side],
+        )
+
     for side in range(2):
         pl.when(has[side])(pos_copy(side).start)
+    for side in range(2):
+        pl.when(has[side])(lig_out(side).start)
 
     def columns(x_row, y_row, at):
         xj[at : at + BLK, :] = jnp.broadcast_to(x_row, (BLK, BLK)).T
         yj[at : at + BLK, :] = jnp.broadcast_to(y_row, (BLK, BLK)).T
 
     for b in range(nblock):
-        columns(rows[b, 0:1, :], rows[b, 1:2, :], RIM + b * BLK)
+        columns(rows[b, 0:1, :], rows[b, 1:2, :], WIDE + b * BLK)
 
     def tile_of(t):
         for q in range(HB):
@@ -178,53 +206,69 @@
                 k_hi[t, at[0], at[1]] = hi
                 k_lo[t, at[0], at[1]] = lo
 
-    lax.fori_loop(1, tiles - 1, lambda t, _: (tile_of(t), 0)[1], 0)
-
-    def log_pairs(which, source, of_ref):
+    lax.fori_loop(2, tiles, lambda t, _: (tile_of(t), 0)[1], 0)
+
+    def log_pairs(which, source, of_ref, at, count):
         pick = jnp.where(
             lax.broadcasted_iota(jnp.int32, (BLK, BLK), 0) == of_ref[...], 1.0, 0.0
         )
         pick = pick.T.astype(jnp.bfloat16)
         pick2 = jnp.concatenate([pick, pick], axis=1)
 
-        @pl.loop(0, tiles)
+        @pl.loop(0, count)
         def _(t):
             here = pl.ds(pl.multiple_of(t * RIM, RIM), RIM)
+            there = pl.ds(pl.multiple_of(t * RIM + at, RIM), RIM)
             x = jnp.concatenate(split(source[here, :]), axis=1)
             picked = lax.dot_general(
                 pick2, x, (((1,), (1,)), ((), ())), preferred_element_type=jnp.float32
             )
-            logs[which, :, here] = POWER * jnp.log(picked)
-
-    lig_of_copy.wait()
-    lig_copy.wait()
-    log_pairs(0, lig, lig_of_ref)
-
-    far = jnp.full((1, BLK), FAR, jnp.float32)
+            logs[which, :, there] = POWER * jnp.log(picked)
+
+    rec_of_copy.wait()
+    rec_copy.wait()
+    log_pairs(1, rec, rec_of_ref, RIM, tiles)
+
     for side in range(2):
-        at = 0 if side == 0 else RIM + cells
+        edge = 0 if side == 0 else WIDE + cells
+        inner = HB if side == 0 else 0
 
         @pl.when(has[side])
         def _():
             pos_arrival(side).wait_recv()
-            for b in range(HB):
-                columns(
-                    pos_recv[side, b, 0:1, :], pos_recv[side, b, 1:2, :], at + b * BLK
-                )
 
         @pl.when(jnp.logical_not(has[side]))
         def _():
-            for b in range(HB):
-                columns(far, far, at + b * BLK)
-
-    lax.fori_loop(0, 2, lambda i, _: (tile_of(i * (tiles - 1)), 0)[1], 0)
-
-    for parity in range(2):
-        for s in range(SETS):
-            for at in (0, RIM + cells):
-                values[parity, s, :, at : at + RIM] = jnp.zeros(
-                    (2 * half, RIM), jnp.bfloat16
-                )
+            pos_recv[side] = jnp.full((REACH, 8, BLK), FAR, jnp.float32)
+            lig[ends[side] : ends[side] + RIM, :] = jnp.ones((RIM, BLK), jnp.float32)
+
+        for b in range(REACH):
+            columns(
+                pos_recv[side, b, 0:1, :], pos_recv[side, b, 1:2, :], edge + b * BLK
+            )
+        for b in range(HB):
+            x = pos_recv[side, inner + b, 0:1, :]
+            own[side * (HB + nblock) + b, 0:1, :] = x
+            own[side * (HB + nblock) + b, 1:2, :] = pos_recv[side, inner + b, 1:2, :]
+            at = ends[side] + b * BLK
+            live[:, at : at + BLK] = jnp.where(x < 0.5 * FAR, 1.0, 0.0)
+
+    lax.fori_loop(0, 2, lambda i, _: (tile_of(i), 0)[1], 0)
+    lax.fori_loop(tiles, tiles + 2, lambda i, _: (tile_of(i), 0)[1], 0)
+
+    lig_of_copy.wait()
+    lig_copy.wait()
+    for side in range(2):
+
+        @pl.when(has[side])
+        def _():
+            lig_arrival(side).wait_recv()
+
+    log_pairs(0, lig, lig_of_ref, 0, tiles + 2)
+
+    for s in range(SETS):
+        for at in (0, WIDE + cells):
+            values[0, s, :, at : at + WIDE] = jnp.zeros((2 * half, WIDE), jnp.bfloat16)
 
     def copy_out(k, s, side):
         return remote(
@@ -246,7 +290,8 @@
 
     def scaled(which, s, t, mass):
         alive = live[:, t * RIM : (t + 1) * RIM]
-        log_have = logs[which, s * half : (s + 1) * half, t * RIM : (t + 1) * RIM]
+        some = pl.ds(pl.multiple_of(s * half, half), half)
+        log_have = logs[which, some, t * RIM : (t + 1) * RIM]
         return alive * jnp.exp2(log_have - POWER * jnp.log(mass + (1.0 - alive)))
 
     def keep(parity, s, t, w):
@@ -255,42 +300,26 @@
         values[parity, s, 0:half, at : at + RIM] = hi
         values[parity, s, half:, at : at + RIM] = lo
 
-    edges = ((0, 0), (1, tiles - 1))
-
     def start(k, s):
-        for side, _ in edges:
+        for side in range(2):
             pl.when(has[side])(copy_out(k, s, side).start)
 
-    def first(t):
+    for t in range(tiles + 2):
         ones = jnp.ones((16, 3 * RIM), jnp.bfloat16)
-        return jnp.dot(ones, k_hi[t], preferred_element_type=jnp.float32)[0:1, :]
-
-    masses = [first(t) for _, t in edges]
-    for s in range(SETS):
-        for side, t in edges:
-            w = scaled(0, s, t, masses[side])
-            send[0, s, side] = w
-            keep(0, s, t, w)
-        start(0, s)
-    for t in range(1, tiles - 1):
-        mass = first(t)
+        mass = jnp.dot(ones, k_hi[t], preferred_element_type=jnp.float32)[0:1, :]
         for s in range(SETS):
-            keep(0, s, t, scaled(0, s, t, mass))
-
-    rec_of_copy.wait()
-    rec_copy.wait()
-    log_pairs(1, rec, rec_of_ref)
-
-    def arrive(k, parity, s):
-        for side, _ in edges:
-            at = 0 if side == 0 else RIM + cells
+            keep(1, s, t, scaled(0, s, t, mass))
+
+    def arrive(k, s):
+        for side in range(2):
+            at = 0 if side == 0 else WIDE + cells
 
             @pl.when(has[side])
             def _():
                 arrival(k, s, side).wait_recv()
                 hi, lo = split(recv[k, s, side])
-                values[parity, s, 0:half, at : at + RIM] = hi
-                values[parity, s, half:, at : at + RIM] = lo
+                values[0, s, 0:half, at : at + WIDE] = hi
+                values[0, s, half:, at : at + WIDE] = lo
 
     def mass_of(parity, s, t):
         both = jnp.dot(
@@ -300,36 +329,28 @@
         )
         return both[0:half] + both[half:]
 
-    def one_round(k, parity):
-        which = 1 - parity
-        for s in range(SETS):
-            arrive(k, parity, s)
-            for side, t in edges:
-                w = scaled(which, s, t, mass_of(parity, s, t))
-                send[k + 1, s, side] = w
-                keep(1 - parity, s, t, w)
-            start(k + 1, s)
-        for s in range(SETS):
-            for t in range(1, tiles - 1):
-                keep(1 - parity, s, t, scaled(which, s, t, mass_of(parity, s, t)))
-
-    def two_rounds(i, carry):
-        one_round(2 * i, 0)
-        one_round(2 * i + 1, 1)
-        return carry
-
-    lax.fori_loop(0, (ROUNDS - 1) // 2, two_rounds, 0)
-
-    last = ROUNDS - 1
-    parity = last % 2
+    def send_side(s, t):
+        keep(1, s, t, scaled(0, s, t, mass_of(0, s, t)))
+
+    def receive_side(k, s):
+        for t in range(1, tiles + 1):
+            w = scaled(1, s, t, mass_of(1, s, t))
+            keep(0, s, t, w)
+            if t <= 2:
+                send[k, s, 0, :, (t - 1) * RIM : t * RIM] = w
+            if t > tiles - 2:
+                at = (t + 1 - tiles) * RIM
+                send[k, s, 1, :, at : at + RIM] = w
+        start(k, s)
 
     def finish(s, t):
-        gathered = mass_of(parity, s, t) + jnp.dot(
-            values[parity, s, 0:half, t * RIM : (t + 3) * RIM],
+        gathered = mass_of(1, s, t) + jnp.dot(
+            values[1, s, 0:half, t * RIM : (t + 3) * RIM],
             k_lo[t],
             preferred_element_type=jnp.float32,
         )
-        flux_t[s * half : (s + 1) * half, t * RIM : (t + 1) * RIM] = (
+        some = pl.ds(pl.multiple_of(s * half, half), half)
+        flux_t[some, (t - 1) * RIM : t * RIM] = (
             scaled(1, s, t, gathered) * gathered
         )
 
@@ -341,16 +362,27 @@
             total = total + jnp.sum(out, axis=0, keepdims=True)
         return total
 
+    pl.loop(0, SETS)(lambda s: receive_side(0, s))
+    for k in range(ROUNDS):
+
+        @pl.loop(0, SETS)
+        def _(s):
+            for t in range(2, tiles):
+                send_side(s, t)
+
+        @pl.loop(0, SETS)
+        def _(s):
+            arrive(k, s)
+            for t in (0, 1, tiles, tiles + 1):
+                send_side(s, t)
+            if k + 1 < ROUNDS:
+                receive_side(k + 1, s)
+            else:
+                for t in range(1, tiles + 1):
+                    finish(s, t)
+
     totals = jnp.zeros((1, BLK), jnp.float32)
-    for t in range(1, tiles - 1):
-        for s in range(SETS):
-            finish(s, t)
-        totals = totals + turn(t)
-    for s in range(SETS):
-        arrive(last, parity, s)
-        for _, t in edges:
-            finish(s, t)
-    for _, t in edges:
+    for t in range(tiles):
         totals = totals + turn(t)
 
     sums[0, 0:1, :] = totals
@@ -377,6 +409,7 @@
         @pl.when(has[side])
         def _():
             pos_copy(side).wait_send()
+            lig_out(side).wait_send()
             for s in range(SETS):
                 for k in range(ROUNDS):
                     copy_out(k, s, side).wait_send()
@@ -396,7 +429,8 @@
     nblock = counts.shape[0]
     tiles = cells // RIM
     pairs = lig_of_pair.shape[0]
-    wide = cells + 2 * RIM
+    inside = cells + 2 * RIM
+    wide = cells + 2 * WIDE
     half = pairs // SETS
     f32, bf16 = jnp.float32, jnp.bfloat16
     vmem = pl.BlockSpec(memory_space=pltpu.VMEM)
@@ -415,26 +449,28 @@
             pltpu.SMEM(counts.shape, jnp.int32),
             pltpu.VMEM((1, pairs), jnp.int32),
             pltpu.VMEM((1, pairs), jnp.int32),
-            pltpu.VMEM(ligands.shape, f32),
+            pltpu.VMEM((inside, ligands.shape[1]), f32),
             pltpu.VMEM(receptors.shape, f32),
+            pltpu.VMEM((nblock + 2 * HB, 8, BLK), f32),
             pltpu.VMEM((nblock, 8, BLK), f32),
-            pltpu.VMEM((nblock, 8, BLK), f32),
-            pltpu.VMEM((2, HB, 8, BLK), f32),
-            pltpu.VMEM((2, HB, 8, BLK), f32),
+            pltpu.VMEM((2, REACH, 8, BLK), f32),
+            pltpu.VMEM((2, REACH, 8, BLK), f32),
             pltpu.VMEM((wide, BLK), f32),
             pltpu.VMEM((wide, BLK), f32),
-            pltpu.VMEM((1, cells), f32),
-            pltpu.VMEM((tiles, 3 * RIM, RIM), bf16),
-            pltpu.VMEM((tiles, 3 * RIM, RIM), bf16),
-            pltpu.VMEM((2, pairs, cells), f32),
+            pltpu.VMEM((1, inside), f32),
+            pltpu.VMEM((tiles + 2, 3 * RIM, RIM), bf16),
+            pltpu.VMEM((tiles + 2, 3 * RIM, RIM), bf16),
+            pltpu.VMEM((2, pairs, inside), f32),
             pltpu.VMEM((2, SETS, 2 * half, wide), bf16),
-            pltpu.VMEM((ROUNDS, SETS, 2, half, RIM), f32),
-            pltpu.VMEM((ROUNDS, SETS, 2, half, RIM), f32),
+            pltpu.VMEM((ROUNDS, SETS, 2, half, WIDE), f32),
+            pltpu.VMEM((ROUNDS, SETS, 2, half, WIDE), f32),
             pltpu.VMEM((pairs, cells), f32),
             pltpu.VMEM((cells, pairs), f32),
             pltpu.VMEM((n, 2, BLK), f32),
             pltpu.SemaphoreType.DMA((6,)),
             pltpu.SemaphoreType.DMA,
+            pltpu.SemaphoreType.DMA((2,)),
+            pltpu.SemaphoreType.DMA((2,)),
             pltpu.SemaphoreType.DMA((2,)),
             pltpu.SemaphoreType.DMA((2,)),
             pltpu.SemaphoreType.DMA((ROUNDS, SETS, 2)),

time: 36.6 us -> 35.5 us (0.970)
  Pallas kernels: 33.8 us -> 32.7 us
    pallas_call x1, Pallas kernels: 33.8 us -> 32.7 us  [body(): pl.pallas_call(functools.partial(kernel, n), out_shape=(jax.ShapeDtypeStr...]
where the time goes in v3:
time: 35.5 us; the launch traced here: 35.3 us
  Pallas kernels  32.7 us (92%)
  other arithmetic  1.87 us (5%)
  local copies, waits for them, and re-layouts  0.66 us (2%)
    pallas_call x1, Pallas kernels, body(): pl.pallas_call(functools.partial(kernel, n), out_shape=(jax.ShapeDtypeStr...  32.7 us
    mul x1, other arithmetic, body(): return flux * scale  1.87 us

profile of v3, /device:TPU:0, one launch (start us, length us, event | category | flops | bytes accessed | tf_op | source)
XLA Modules:
  0.0 35.3 jit_solution(14711281218345011299)
XLA Ops:
  0.0 32.7 %shard_map.64 = (f32[1024,128]{1,0:T(8,128)}, f32[1,128]{1,0:T(1,128)}) custom-call(f32[2,1024]{1,0:T(2,128)} %pos_hbm.1, s32[8]{0:T(128)} %counts_hbm.1, s32[1,128]{1,0:T(1,128)} %bitcast.3, s32[1,128]{1,0:T(1,128)} %bitcast.4, f32[1024,128]{1,0:T(8,128)} %lig_hbm.1, f32[1024,128]{1,0:T(8,128)} %rec_hbm.1), custom_call_target="tpu_custom_call" | custom-call | tf_op jit(solution)/shard_map/pallas_call | solution.py:439
  32.7 0.0 copy-start
  32.8 0.7 %copy-done = f32[1,128]{1,0:T(1,128)S(1)} copy-done((f32[1,128]{1,0:T(1,128)S(1)}, f32[1,128]{1,0:T(1,128)}, u32[]{:S(2)}) %copy-start) | copy-done | bytes 536
  33.4 1.9 %broadcast_multiply_fusion = f32[1024,128]{1,0:T(8,128)} fusion(f32[1024,128]{1,0:T(8,128)} %get-tuple-element.7, f32[128]{0:T(128)S(1)} %bitcast.5), kind=kLoop, calls=%fused_computation | loop fusion | flops 131072 | bytes 1049088 | tf_op jit(solution)/shard_map/mul | solution.py:492
Async XLA Ops:
  32.7 0.7 %copy-start = (f32[1,128]{1,0:T(1,128)S(1)}, f32[1,128]{1,0:T(1,128)}, u32[]{:S(2)}) copy-start(f32[1,128]{1,0:T(1,128)} %get-tuple-element.8) | copy-start | bytes 1540

commit v4 on v3

--- a/solution.py
+++ b/solution.py
@@ -421,6 +421,10 @@
     whole = jnp.sum(sums[...], axis=0)
     scale_ref[0:1, :] = whole[1:2, :] / whole[0:1, :]
     out_copy.wait()
+
+
+def scale_kernel(flux_ref, scale_ref, out_ref):
+    out_ref[...] = flux_ref[...] * scale_ref[...]
 
 
 def body(positions, counts, ligands, receptors, lig_of_pair, rec_of_pair):
@@ -489,7 +493,17 @@
         ligands,
         receptors,
     )
-    return flux * scale
+    step = cells // 2
+    return pl.pallas_call(
+        scale_kernel,
+        grid=(cells // step,),
+        out_shape=jax.ShapeDtypeStruct((cells, pairs), f32),
+        in_specs=[
+            pl.BlockSpec((step, pairs), lambda i: (i, 0)),
+            pl.BlockSpec((1, pairs), lambda i: (0, 0)),
+        ],
+        out_specs=pl.BlockSpec((step, pairs), lambda i: (i, 0)),
+    )(flux, scale)
 
 
 def solution(mesh):

time: 35.5 us -> 34.6 us (0.975)
  other arithmetic: 1.87 us -> 0 us
  Pallas kernels: 32.7 us -> 34.4 us
  local copies, waits for them, and re-layouts: 0.66 us -> 0 us
    mul x1 -> x0, other arithmetic: 1.87 us -> none  [body(): return flux * scale]
    pallas_call x0 -> x1, Pallas kernels: none -> 1.77 us  [body(): pl.pallas_call(scale_kernel, grid=(cells // step,), out_shape=jax.ShapeDt...]
    unnamed x2 -> x0, local copies, waits for them, and re-layouts: 0.66 us -> none
where the time goes in v4:
time: 34.6 us; the launch traced here: 34.4 us
  Pallas kernels  34.4 us (99%)
    pallas_call x1, Pallas kernels, body(): pl.pallas_call(functools.partial(kernel, n), out_shape=(jax.ShapeDtypeStr...  32.7 us
    pallas_call x1, Pallas kernels, body(): pl.pallas_call(scale_kernel, grid=(cells // step,), out_shape=jax.ShapeDt...  1.77 us

profile of v4, /device:TPU:0, one launch (start us, length us, event | category | flops | bytes accessed | tf_op | source)
XLA Modules:
  0.0 34.4 jit_solution(11197543600548901351)
XLA Ops:
  0.0 32.7 %shard_map.64 = (f32[1024,128]{1,0:T(8,128)}, f32[1,128]{1,0:T(1,128)}) custom-call(f32[2,1024]{1,0:T(2,128)} %pos_hbm.1, s32[8]{0:T(128)} %counts_hbm.1, s32[1,128]{1,0:T(1,128)} %bitcast.2, s32[1,128]{1,0:T(1,128)} %bitcast.3, f32[1024,128]{1,0:T(8,128)} %lig_hbm.1, f32[1024,128]{1,0:T(8,128)} %rec_hbm.1), custom_call_target="tpu_custom_call" | custom-call | tf_op jit(solution)/shard_map/pallas_call | solution.py:443
  32.7 1.8 %shard_map.65 = f32[1024,128]{1,0:T(8,128)} custom-call(f32[1024,128]{1,0:T(8,128)} %get-tuple-element.7.flux_ref, f32[1,128]{1,0:T(1,128)} %get-tuple-element.8.scale_ref), custom_call_target="tpu_custom_call" | custom-call | tf_op jit(solution)/shard_map/pallas_call | solution.py:497
